TPU v7x, 32 devices: a whole 2x2x4 slice. The times are simulated.
32 devices in a mesh: grp: 2 (over y), lon: 4 (over x, core), lat: 4 (over z).
Axes of the slice: x: 2, y: 2, z: 4, core: 2. Of those that a mesh axis runs over, the one named last changes fastest.
Arguments:
- grid_field: bfloat16 [192, 1440, 256], P(('grp', 'lat'), 'lon'), parts along dimension 0, may hold values from -6 to 6
- weights: bfloat16 [512, 2, 256, 256], P(('lon', 'lat')), may hold values from -0.25 to 0.25
Outputs:
- upsampled: bfloat16 [192, 2880, 256], P(('grp', 'lat'), 'lon'), parts along dimension 0
There are 2 independent parts, one for each index of `grp`. A program takes and returns all parts, laid end to end along the dimension named above; an argument that names none is the same for every part. Nothing has to cross between parts.
All inputs are finite; a program needn't handle non-finite values.
Results may differ from a plain program's by a relative error of at most 0.014.
Values may be sent and summed in bfloat16 or wider, within the bound.
A program may use at most 320 MiB of HBM per device.

v0:
```python
import math

import jax
import jax.numpy as jnp
from jax import lax
from jax.sharding import PartitionSpec as P

NLON = 1440
M = 512


def analysis_table(lon_index):
    mode_index = jnp.arange(M, dtype=jnp.int32)
    norm_scale = 1.0 / math.sqrt(NLON)
    phase_index = mode_index[:, None] * lon_index[None, :] % NLON
    angles = 2.0 * math.pi / NLON * phase_index.astype(jnp.float32)
    table = jnp.stack([jnp.cos(angles) * norm_scale, -jnp.sin(angles) * norm_scale], 1)
    return table.reshape(2 * M, lon_index.shape[0]).astype(jnp.bfloat16)


def synthesis_table(out_index):
    mode_index = jnp.arange(M, dtype=jnp.int32)
    norm_scale = 1.0 / math.sqrt(NLON)
    phase_out = mode_index[:, None] * out_index[None, :] % (2 * NLON)
    angles_out = 2.0 * math.pi / (2 * NLON) * phase_out.astype(jnp.float32)
    factor = jnp.where(mode_index == 0, 1.0, 2.0).astype(jnp.float32)[:, None] * norm_scale
    table = jnp.stack([jnp.cos(angles_out) * factor, -jnp.sin(angles_out) * factor], 1)
    return table.reshape(2 * M, out_index.shape[0]).astype(jnp.bfloat16)


def mix_modes(slab_modes, portion):
    re_part = portion[:, 0]
    im_part = portion[:, 1]
    wide_weight = jnp.stack(
        [jnp.concatenate([re_part, im_part], -1), jnp.concatenate([-im_part, re_part], -1)], 1
    )
    return jnp.einsum(
        "mplc,mpcd->mld", slab_modes, wide_weight, preferred_element_type=jnp.float32
    ).astype(jnp.bfloat16)


def on_device(grid_field, weights):
    lat_rows, lon_dev, channels = grid_field.shape
    lon_count = lax.axis_size("lon")
    lon_rank = lax.axis_index("lon")
    modes_dev = M // lon_count
    lon_index = lon_rank * lon_dev + jnp.arange(lon_dev, dtype=jnp.int32)
    fwd_local = analysis_table(lon_index)
    table_rows = fwd_local
    summed = lax.psum_scatter(
        jnp.einsum(
            "kn,lnc->klc", table_rows, grid_field, preferred_element_type=jnp.float32
        ).astype(jnp.bfloat16),
        "lon",
        scatter_dimension=0,
        tiled=True,
    )
    lat_count = lax.axis_size("lat")
    own_modes = modes_dev // lat_count
    moved = lax.all_to_all(
        summed.reshape(lat_count, 2 * own_modes, lat_rows, channels), "lat", 0, 0, tiled=True
    )
    spectrum = (
        moved.reshape(lat_count, own_modes, 2, lat_rows, channels)
        .transpose(1, 2, 0, 3, 4)
        .reshape(own_modes, 2, lat_count * lat_rows, channels)
    )
    mixed_own = mix_modes(spectrum, weights)
    back = mixed_own.reshape(own_modes, lat_count, lat_rows, 2 * channels).transpose(1, 0, 2, 3)
    mixed_spec = lax.all_to_all(back, "lat", 0, 0, tiled=True).reshape(
        modes_dev, lat_rows, 2 * channels
    )
    out_dev = 2 * NLON // lon_count
    out_index = lon_rank * out_dev + jnp.arange(out_dev, dtype=jnp.int32)
    inv_local = synthesis_table(out_index).reshape(M, 2, out_dev)
    portion = lax.all_gather(mixed_spec, "lon", axis=0, tiled=True)
    count = portion.shape[0]
    table_rows = inv_local
    parted = portion.reshape(count, lat_rows, 2, channels)
    running = jnp.einsum("mlpc,mpn->lnc", parted, table_rows, preferred_element_type=jnp.float32)
    return running.astype(jnp.bfloat16)


def solution(mesh):
    placed = (P(("grp", "lat"), "lon", None), P(("lon", "lat"), None, None, None))
    return jax.shard_map(
        on_device,
        mesh=mesh,
        in_specs=placed,
        out_specs=P(("grp", "lat"), "lon", None),
        check_vma=False,
    )
```

profile of v0, /device:TPU:13, one launch (start us, length us, event | category | flops | bytes accessed | tf_op | source)
XLA Modules:
  0.0 408.0 jit_solution(5694878123159895570)
XLA Ops:
  6.5 0.0 reduce-scatter.2.cloned.1.call-start
  6.5 3.6 multiply_convert_fusion.3
  10.1 0.1 pad_maximum_fusion
  10.2 1.2 copy.24
  11.4 0.6 convert_element_type.48
  12.1 11.8 %convolution_convert_fusion = bf16[1024,24,256]{2,0,1:T(8,128)(2,1)} fusion(bf16[24,360,256]{2,1,0:T(8,128)(2,1)} %param.2, bf16[1024,360]{1,0:T(8,128)(2,1)S(1)} %convert_element_type.48), kind=kOutput, calls=%fused_computation.8 | convolution fusion | flops 4536139776 | bytes 17743872 | tf_op jit(solution)/shard_map/kn,lnc->klc/dot_general | solution.py:51
  23.9 0.0 reduce-scatter.2.cloned.1.call-update
  23.9 100.3 %reduce-scatter.2.cloned.1.call-done = bf16[256,24,256]{2,0,1:T(8,128)(2,1)} async-done(((bf16[1024,24,256]{2,0,1:T(8,128)(2,1)}), bf16[256,24,256]{2,0,1:T(8,128)(2,1)}) %reduce-scatter.2.cloned.1.call-update) | async-done | bytes 3145744 | tf_op jit(solution)/shard_map/reduce_scatter | solution.py:50
  124.2 4.0 copy.26
  128.3 4.6 %all-to-all-start = ((bf16[4,64,24,256]{3,1,2,0:T(8,128)(2,1)}), bf16[4,64,24,256]{3,1,2,0:T(8,128)(2,1)S(1)}, u32[]{:S(2)}, u32[]{:S(2)}) async-start(bf16[4,64,24,256]{3,1,2,0:T(8,128)(2,1)} %copy.26), calls=%async_computation.1 | async-start | bytes 6291456 | tf_op jit(solution)/shard_map/all_to_all | solution.py:60
  132.8 0.0 all-gather.2.cloned.1.call-start
  132.8 2.5 fusion.22
  135.3 3.8 slice_bitcast_fusion
  139.2 6.3 %maximum_bitcast_fusion = (bf16[32,1,256,512]{3,2,1,0:T(8,128)(2,1)}, bf16[32,1,256,512]{3,2,1,0:T(8,128)(2,1)}) fusion(bf16[32,256,256]{2,1,0:T(8,128)(2,1)S(1)} %get-tuple-element.5, bf16[32,256,256]{2,1,0:T(8,128)(2,1)S(1)} %get-tuple-element.6, bf16[32,256,256]{2,1,0:T(8,128)(2,1)S(1)} %fusion.22), kind=kLoop, calls=%fused_computation.6 | loop fusion | flops 33554432 | bytes 29360128 | tf_op jit(solution)/shard_map/stack | solution.py:34
  145.4 54.1 %all-to-all-done = bf16[4,64,24,256]{3,1,2,0:T(8,128)(2,1)S(1)} async-done(((bf16[4,64,24,256]{3,1,2,0:T(8,128)(2,1)}), bf16[4,64,24,256]{3,1,2,0:T(8,128)(2,1)S(1)}, u32[]{:S(2)}, u32[]{:S(2)}) %all-to-all-start) | async-done | bytes 3145760 | tf_op jit(solution)/shard_map/all_to_all | solution.py:60
  199.6 1.8 copy.39
  201.3 7.5 %bitcast_convert_fusion.1 = bf16[32,96,512]{2,1,0:T(8,128)(2,1)S(1)} fusion(bf16[32,2,96,256]{3,2,1,0:T(8,128)(2,1)S(1)} %bitcast.51, bf16[32,1,256,512]{3,2,1,0:T(8,128)(2,1)} %get-tuple-element.8, bf16[32,1,256,512]{3,2,1,0:T(8,128)(2,1)} %get-tuple-element.7), kind=kOutput, calls=%fused_computation.9 | convolution fusion | flops 1620574208 | bytes 23068672 | tf_op jit(solution)/shard_map/mplc,mpcd->mld/dot_general | solution.py:37
  208.9 0.2 copy.43
  209.1 74.7 %all_to_all.10 = bf16[4,32,24,512]{3,2,1,0:T(8,128)(2,1)} all-to-all(bf16[4,32,24,512]{3,2,1,0:T(8,128)(2,1)S(1)} %bitcast.49), channel_id=1, replica_groups=mesh['grp'=2,'lon'=4,'lat'=4] {'lat'}, dimensions={0} | all-to-all | bytes 6291456 | tf_op jit(solution)/shard_map/all_to_all | solution.py:70
  283.9 0.0 all-gather.2.cloned.1.call-update
  283.9 6.9 %multiply_convert_fusion.1 = (bf16[512,1,720]{0,2,1:T(8,128)(2,1)S(1)}, bf16[512,1,720]{0,2,1:T(8,128)(2,1)S(1)}) fusion(f32[512]{0:T(512)S(1)} %select_multiply_fusion, s32[720]{0:T(1024)S(1)} %iota_add_fusion), kind=kLoop, calls=%fused_computation.20 | loop fusion | flops 5160960 | bytes 1479488 | tf_op jit(solution)/shard_map/convert.2
  290.8 76.7 %all-gather.2.cloned.1.call-done = bf16[512,24,512]{2,1,0:T(8,128)(2,1)} async-done(((bf16[128,24,512]{2,1,0:T(8,128)(2,1)}), bf16[512,24,512]{2,1,0:T(8,128)(2,1)}) %all-gather.2.cloned.1.call-update) | async-done | bytes 12582928 | tf_op jit(solution)/shard_map/all_gather | solution.py:76
  367.5 17.1 %copy.32 = bf16[512,24,512]{0,2,1:T(8,128)(2,1)} copy(bf16[512,24,512]{2,1,0:T(8,128)(2,1)} %all-gather.2.cloned.1.call-done) | data formatting | bytes 25165824 | tf_op jit(solution)/shard_map/all_gather | solution.py:76
  384.6 16.5 %fusion.4 = bf16[24,720,256]{2,1,0:T(8,128)(2,1)} fusion(bf16[512,24,2,256]{0,3,2,1:T(8,128)(2,1)} %bitcast.47, bf16[512,1,720]{0,2,1:T(8,128)(2,1)S(1)} %get-tuple-element.10, bf16[512,1,720]{0,2,1:T(8,128)(2,1)S(1)} %get-tuple-element.9), kind=kOutput, calls=%fused_computation.5 | convolution fusion | flops 9067069440 | bytes 22904832 | tf_op jit(solution)/shard_map/mlpc,mpn->lnc/dot_general | solution.py:80
  (3 shorter events, 0.0 us)
Async XLA Ops:
  6.5 117.7 %reduce-scatter.2.cloned.1.call-start = ((), (), s32[]{:S(2)}) async-start(), calls=%async_computation.3 | async-start | bytes 15728640 | tf_op jit(solution)/shard_map/reduce_scatter | solution.py:50
  128.3 71.3 %all-to-all-start = ((bf16[4,64,24,256]{3,1,2,0:T(8,128)(2,1)}), bf16[4,64,24,256]{3,1,2,0:T(8,128)(2,1)S(1)}, u32[]{:S(2)}, u32[]{:S(2)}) async-start(bf16[4,64,24,256]{3,1,2,0:T(8,128)(2,1)} %copy.26), calls=%async_computation.1 | async-start | bytes 6291456 | tf_op jit(solution)/shard_map/all_to_all | solution.py:60
  132.8 234.7 %all-gather.2.cloned.1.call-start = ((), (), s32[]{:S(2)}) async-start(), calls=%async_computation.4 | async-start | bytes 15728640 | tf_op jit(solution)/shard_map/all_gather | solution.py:76
Sparse Core Ops, SparseCore 0:
  24.0 100.1 reduce-scatter.1
  284.0 83.4 all-gather.1
where the time goes:
time: 410 us; the launch traced here: 408 us
  waiting for transfers between devices  231 us (56%)
  blocking collectives  74.7 us (18%)
  matrix products  35.9 us (9%)
  local copies, waits for them, and re-layouts  28.9 us (7%)
  other arithmetic  19.3 us (5%)
  between operations  13.5 us (3%)
  starting transfers between devices  4.57 us (1%)
    reduce_scatter x1, waiting for transfers between devices, on_device(): lax.psum_scatter(jnp.einsum('kn,lnc->klc', table_rows, grid_field, prefer...  100 us
    all_gather x1, waiting for transfers between devices, on_device(): portion = lax.all_gather(mixed_spec, 'lon', axis=0, tiled=True)  76.7 us
    all_to_all x1, blocking collectives, on_device(): lax.all_to_all(back, 'lat', 0, 0, tiled=True)  74.7 us
    all_to_all x1, waiting for transfers between devices, on_device(): lax.all_to_all(summed.reshape(lat_count, 2 * own_modes, lat_rows, channel...  54.1 us
    all_gather x1, local copies, waits for them, and re-layouts, on_device(): portion = lax.all_gather(mixed_spec, 'lon', axis=0, tiled=True)  17.1 us
    dot_general x1, matrix products, on_device(): jnp.einsum('mlpc,mpn->lnc', parted, table_rows, preferred_element_type=jn...  16.5 us
    dot_general x1, matrix products, on_device(): jnp.einsum('kn,lnc->klc', table_rows, grid_field, preferred_element_type=...  11.8 us
    another operation x2, other arithmetic  10.5 us
  transfers between devices with their start and end apart: 3, of which 3 were waited for; matrix products, arithmetic and copies ran while one was open for 5% of the time, Pallas kernels for 0%

commit v1 on v0

--- a/solution.py
+++ b/solution.py
@@ -2,11 +2,16 @@
 
 import jax
 import jax.numpy as jnp
+import numpy as np
 from jax import lax
+from jax.experimental import pallas as pl
+from jax.experimental.pallas import tpu as pltpu
 from jax.sharding import PartitionSpec as P
 
 NLON = 1440
 M = 512
+ROWS = 16
+HALVES = 2
 
 
 def analysis_table(lon_index):
@@ -45,11 +50,12 @@
     lon_rank = lax.axis_index("lon")
     modes_dev = M // lon_count
     lon_index = lon_rank * lon_dev + jnp.arange(lon_dev, dtype=jnp.int32)
-    fwd_local = analysis_table(lon_index)
-    table_rows = fwd_local
     summed = lax.psum_scatter(
         jnp.einsum(
-            "kn,lnc->klc", table_rows, grid_field, preferred_element_type=jnp.float32
+            "kn,lnc->klc",
+            analysis_table(lon_index),
+            grid_field,
+            preferred_element_type=jnp.float32,
         ).astype(jnp.bfloat16),
         "lon",
         scatter_dimension=0,
@@ -75,16 +81,302 @@
     inv_local = synthesis_table(out_index).reshape(M, 2, out_dev)
     portion = lax.all_gather(mixed_spec, "lon", axis=0, tiled=True)
     count = portion.shape[0]
-    table_rows = inv_local
     parted = portion.reshape(count, lat_rows, 2, channels)
-    running = jnp.einsum("mlpc,mpn->lnc", parted, table_rows, preferred_element_type=jnp.float32)
+    running = jnp.einsum("mlpc,mpn->lnc", parted, inv_local, preferred_element_type=jnp.float32)
     return running.astype(jnp.bfloat16)
+
+
+def host_tables(lon_count, lat_count, chunks):
+    mode = np.arange(M, dtype=np.int32)[:, None]
+    scale = 1.0 / math.sqrt(NLON)
+    turn = np.float32(2.0 * math.pi / NLON)
+    angle = turn * (mode * np.arange(NLON, dtype=np.int32)[None] % NLON).astype(np.float32)
+    ana = np.stack([np.cos(angle) * scale, -np.sin(angle) * scale], 1)
+    ana = ana.reshape(lon_count, lat_count, chunks, ROWS, lon_count, NLON // lon_count)
+    ana = ana.transpose(4, 0, 2, 1, 3, 5).reshape(
+        lon_count, lon_count, chunks, lat_count * ROWS, NLON // lon_count
+    )
+    turn = np.float32(2.0 * math.pi / (2 * NLON))
+    angle = turn * (mode * np.arange(2 * NLON, dtype=np.int32)[None] % (2 * NLON)).astype(np.float32)
+    factor = np.where(mode == 0, 1.0, 2.0).astype(np.float32) * np.float32(scale)
+    syn = np.stack([np.cos(angle) * factor, -np.sin(angle) * factor], 1)
+    syn = syn.reshape(lon_count, lat_count, chunks, ROWS, lon_count, 2 * NLON // lon_count)
+    syn = syn.transpose(4, 5, 2, 0, 1, 3).reshape(lon_count, 2 * NLON // lon_count, 2 * M)
+    kind = jnp.bfloat16
+    return ana.astype(np.float32).astype(kind), syn.astype(np.float32).astype(kind)
+
+
+def spectral_kernel(
+    lats, lat_n, chunks,
+    grid_in, w_in, tab_in, full,
+    g_own, g_peer, w_buf, tab, xs, acc, xr, zr, ys, xt, yt,
+    local_sem, place_sem, gs, gr, x_s, x_r, z_s, z_r, y_s, y_r, a_s, a_r, b_s, b_r, f_s, f_r,
+):
+    lon = lax.axis_index("lon")
+    z = lax.axis_index("lat")
+    core = lon % 2
+    side = lon // 2
+    x_lon = (1 - side) * 2 + core
+    mate_lon = side * 2 + 1 - core
+    x_peer = {"lon": x_lon}
+    mate = {"lon": mate_lon}
+    mesh_id = pl.DeviceIdType.MESH
+    part = lats // HALVES
+
+    def far(src, dst, send, recv, peer):
+        return pltpu.make_async_remote_copy(
+            src_ref=src, dst_ref=dst, send_sem=send, recv_sem=recv,
+            device_id=peer, device_id_type=mesh_id,
+        )
+
+    loads = []
+    for i, block in enumerate((lon, mate_lon)):
+        for j, owner in enumerate((x_lon, lon)):
+            loads.append(
+                pltpu.make_async_copy(
+                    tab_in.at[block, owner], tab.at[i, j], local_sem.at[2 * i + j]
+                )
+            )
+    loads.append(pltpu.make_async_copy(grid_in, g_own, local_sem.at[4]))
+    w_load = pltpu.make_async_copy(w_in, w_buf, local_sem.at[5])
+    for copy in loads:
+        copy.start()
+
+    barrier = pltpu.get_barrier_semaphore()
+    for peer in [mate, x_peer] + [{"lat": (z + d) % lat_n} for d in range(1, lat_n)]:
+        pl.semaphore_signal(barrier, inc=1, device_id=peer, device_id_type=mesh_id)
+    pl.semaphore_wait(barrier, 1 + lat_n)
+
+    g_copy = [
+        far(grid_in.at[pl.ds(h * part, part)], g_peer.at[pl.ds(h * part, part)], gs.at[h], gr.at[h], mate)
+        for h in range(HALVES)
+    ]
+    for copy in g_copy:
+        copy.start()
+    w_load.start()
+    for copy in loads:
+        copy.wait()
+
+    def half(ref, k, h):
+        return ref.at[k, :, pl.ds(h * part, part)]
+
+    def x_copy(k, h):
+        return far(half(xs, k, h), half(xr, k, h), x_s.at[k, h], x_r.at[k, h], x_peer)
+
+    def analyse(k):
+        for h in range(HALVES):
+            if k == 0:
+                g_copy[h].wait_recv()
+
+            @pl.loop(h * part, (h + 1) * part)
+            def _(l):
+                for j, out in ((0, xs), (1, acc)):
+                    value = jnp.dot(tab[0, j, k], g_own[l], preferred_element_type=jnp.float32)
+                    value += jnp.dot(tab[1, j, k], g_peer[l], preferred_element_type=jnp.float32)
+                    value = value.astype(jnp.bfloat16)
+                    for owner in range(lat_n):
+                        out[k, owner, l] = value[owner * ROWS:(owner + 1) * ROWS]
+
+            x_copy(k, h).start()
+
+    def z_copy(k, h, d, sending):
+        source = z if sending else (z - d + lat_n) % lat_n
+        target = (z + d) % lat_n if sending else z
+        return far(
+            acc.at[k, target, pl.ds(h * part, part)],
+            zr.at[k, pl.ds(source * lats + h * part, part)],
+            z_s.at[k, h, d - 1], z_r.at[k, h, d - 1], {"lat": (z + d) % lat_n},
+        )
+
+    def add_up(k):
+        for h in range(HALVES):
+            x_copy(k, h).wait_recv()
+
+            @pl.loop(h * part, (h + 1) * part)
+            def _(l):
+                for owner in range(lat_n):
+                    value = acc[k, owner, l].astype(jnp.float32) + xr[k, owner, l].astype(jnp.float32)
+                    acc[k, owner, l] = value.astype(jnp.bfloat16)
+
+            for d in range(1, lat_n):
+                z_copy(k, h, d, True).start()
+
+            @pl.loop(0, part)
+            def _(l):
+                zr[k, z * lats + h * part + l] = acc[k, z, h * part + l]
+
+    def y_copy(k, d, sending):
+        source = z if sending else (z - d + lat_n) % lat_n
+        target = (z + d) % lat_n if sending else z
+        return far(
+            ys.at[k, pl.ds(target * lats, lats)],
+            full.at[:, pl.ds((k * 4 + lon) * lat_n * ROWS + source * ROWS, ROWS)],
+            y_s.at[k, d - 1], y_r.at[k, d - 1], {"lat": (z + d) % lat_n},
+        )
+
+    def place(k):
+        return pltpu.make_async_copy(
+            ys.at[k, pl.ds(z * lats, lats)],
+            full.at[:, pl.ds((k * 4 + lon) * lat_n * ROWS + z * ROWS, ROWS)],
+            place_sem.at[k],
+        )
+
+    tiles = lat_n * lats // 16
+
+    def mix(k):
+        for h in range(HALVES):
+            for d in range(1, lat_n):
+                z_copy(k, h, d, False).wait_recv()
+        if k == 0:
+            w_load.wait()
+
+        @pl.loop(0, tiles)
+        def _(t):
+            start = pl.multiple_of(t * 16, 16)
+            value = zr[k, pl.ds(start, 16)].astype(jnp.float32)
+            xt[:, pl.ds(start, 16)] = jnp.swapaxes(value, 0, 1).astype(jnp.bfloat16)
+
+        rows = lat_n * lats
+
+        @pl.loop(0, ROWS // 2)
+        def _(i):
+            both = xt[pl.ds(2 * i, 2)].reshape(2 * rows, xt.shape[-1])
+            by_re = jnp.dot(both, w_buf[k * (ROWS // 2) + i, 0], preferred_element_type=jnp.float32)
+            by_im = jnp.dot(both, w_buf[k * (ROWS // 2) + i, 1], preferred_element_type=jnp.float32)
+            yt[2 * i] = (by_re[:rows] - by_im[rows:]).astype(jnp.bfloat16)
+            yt[2 * i + 1] = (by_im[:rows] + by_re[rows:]).astype(jnp.bfloat16)
+
+        @pl.loop(0, tiles)
+        def _(t):
+            start = pl.multiple_of(t * 16, 16)
+            value = yt[:, pl.ds(start, 16)].astype(jnp.float32)
+            ys[k, pl.ds(start, 16)] = jnp.swapaxes(value, 0, 1).astype(jnp.bfloat16)
+
+        for d in range(1, lat_n):
+            y_copy(k, d, True).start()
+        place(k).start()
+
+    def block(k, owner):
+        return full.at[:, pl.ds((k * 4 + owner) * lat_n * ROWS, lat_n * ROWS)]
+
+    def across(k, sending):
+        at = block(k, lon if sending else x_lon)
+        return far(at, at, a_s.at[k], a_r.at[k], x_peer)
+
+    def beside(k, sending):
+        at = block(k, lon if sending else mate_lon)
+        return far(at, at, b_s.at[k], b_r.at[k], mate)
+
+    def onward(k, sending):
+        at = block(k, x_lon if sending else 3 - lon)
+        return far(at, at, f_s.at[k], f_r.at[k], mate)
+
+    def spread(k):
+        for d in range(1, lat_n):
+            y_copy(k, d, False).wait_recv()
+        place(k).wait()
+        across(k, True).start()
+        beside(k, True).start()
+
+    def forward(k):
+        across(k, False).wait_recv()
+        onward(k, True).start()
+
+    steps = []
+    for k in range(chunks):
+        steps += [(2 * k, 0, analyse, k), (2 * k + 3, 1, add_up, k), (2 * k + 6, 2, mix, k)]
+        steps += [(2 * k + 9, 3, spread, k), (2 * k + 12, 4, forward, k)]
+    for _, _, stage, k in sorted(steps, key=lambda s: (s[0], -s[1])):
+        stage(k)
+
+    for h in range(HALVES):
+        g_copy[h].wait_send()
+    for k in range(chunks):
+        for h in range(HALVES):
+            x_copy(k, h).wait_send()
+            for d in range(1, lat_n):
+                z_copy(k, h, d, True).wait_send()
+        for d in range(1, lat_n):
+            y_copy(k, d, True).wait_send()
+        across(k, True).wait_send()
+        beside(k, True).wait_send()
+        beside(k, False).wait_recv()
+        onward(k, True).wait_send()
+        onward(k, False).wait_recv()
+
+
+def synthesis_kernel(table, spectrum, out):
+    out[0] = jnp.dot(table[...], spectrum[0], preferred_element_type=jnp.float32).astype(out.dtype)
+
+
+def fast_device(grid_field, weights, ana, syn):
+    lats, lon_dev, channels = grid_field.shape
+    lat_n = lax.axis_size("lat")
+    modes = weights.shape[0]
+    chunks = 2 * modes // ROWS
+    kind = jnp.bfloat16
+    dma = pltpu.SemaphoreType.DMA
+    chunk = pltpu.VMEM((chunks, lat_n, lats, ROWS, channels), kind)
+    owned = pltpu.VMEM((chunks, lat_n * lats, ROWS, channels), kind)
+    turned = pltpu.VMEM((ROWS, lat_n * lats, channels), kind)
+    pair = dma((chunks, HALVES))
+    line = dma((chunks,))
+
+    def kernel(*refs):
+        spectral_kernel(lats, lat_n, chunks, *refs)
+
+    full = pl.pallas_call(
+        kernel,
+        out_shape=jax.ShapeDtypeStruct((lats, 2 * M, channels), kind),
+        in_specs=[pl.BlockSpec(memory_space=pl.ANY)] * 3,
+        out_specs=pl.BlockSpec(memory_space=pl.ANY),
+        scratch_shapes=[
+            pltpu.VMEM((lats, lon_dev, channels), kind),
+            pltpu.VMEM((lats, lon_dev, channels), kind),
+            pltpu.VMEM(weights.shape, kind),
+            pltpu.VMEM((2, 2) + ana.shape[2:], kind),
+            chunk, chunk, chunk, owned, owned, turned, turned,
+            dma((6,)), line, dma((HALVES,)), dma((HALVES,)),
+            pair, pair,
+            dma((chunks, HALVES, lat_n - 1)), dma((chunks, HALVES, lat_n - 1)),
+            dma((chunks, lat_n - 1)), dma((chunks, lat_n - 1)),
+            line, line, line, line, line, line,
+        ],
+        compiler_params=pltpu.CompilerParams(
+            collective_id=0, has_side_effects=True, vmem_limit_bytes=56 * 2**20
+        ),
+        cost_estimate=pl.CostEstimate(
+            flops=8 * 10**9, bytes_accessed=40 * 2**20, transcendentals=0
+        ),
+    )(grid_field, weights, ana)
+    table = lax.dynamic_index_in_dim(syn, lax.axis_index("lon"), 0, keepdims=False)
+    out_dev = table.shape[0]
+    return pl.pallas_call(
+        synthesis_kernel,
+        grid=(lats,),
+        out_shape=jax.ShapeDtypeStruct((lats, out_dev, channels), kind),
+        in_specs=[
+            pl.BlockSpec(table.shape, lambda l: (0, 0)),
+            pl.BlockSpec((1, 2 * M, channels), lambda l: (l, 0, 0)),
+        ],
+        out_specs=pl.BlockSpec((1, out_dev, channels), lambda l: (l, 0, 0)),
+        compiler_params=pltpu.CompilerParams(vmem_limit_bytes=40 * 2**20),
+    )(table, full)
 
 
 def solution(mesh):
     placed = (P(("grp", "lat"), "lon", None), P(("lon", "lat"), None, None, None))
+    lon_count, lat_count = mesh.shape["lon"], mesh.shape["lat"]
+    owned_rows = 2 * M // (lon_count * lat_count)
+    body = on_device
+    if lon_count == 4 and lat_count == 4 and owned_rows % ROWS == 0:
+        ana, syn = host_tables(lon_count, lat_count, owned_rows // ROWS)
+
+        def body(grid_field, weights):
+            return fast_device(grid_field, weights, jnp.asarray(ana), jnp.asarray(syn))
+
     return jax.shard_map(
-        on_device,
+        body,
         mesh=mesh,
         in_specs=placed,
         out_specs=P(("grp", "lat"), "lon", None),

time: 410 us -> 211 us (0.51)
  waiting for transfers between devices: 231 us -> 0 us
  Pallas kernels: 0 us -> 205 us
  blocking collectives: 74.7 us -> 0 us
  matrix products: 35.9 us -> 0 us
  local copies, waits for them, and re-layouts: 28.9 us -> 6.05 us
  other arithmetic: 19.3 us -> 0 us
  between operations: 13.5 us -> 0.02 us
  starting transfers between devices: 4.57 us -> 0 us
    pallas_call x0 -> x2, Pallas kernels: none -> 205 us  [the longest x1 189 us: fast_device(): pl.pallas_call(kernel, out_shape=jax.ShapeDtypeStruct((lats, 2 * M, chann...]
    reduce_scatter x1 -> x0, waiting for transfers between devices: 100 us -> none  [on_device(): lax.psum_scatter(jnp.einsum('kn,lnc->klc', table_rows, grid_field, prefer...]
    all_gather x1 -> x0, waiting for transfers between devices: 76.7 us -> none  [on_device(): portion = lax.all_gather(mixed_spec, 'lon', axis=0, tiled=True)]
    all_to_all x1 -> x0, blocking collectives: 74.7 us -> none  [on_device(): lax.all_to_all(back, 'lat', 0, 0, tiled=True)]
    all_to_all x1 -> x0, waiting for transfers between devices: 54.1 us -> none  [on_device(): lax.all_to_all(summed.reshape(lat_count, 2 * own_modes, lat_rows, channel...]
    dot_general x3 -> x0, matrix products: 35.9 us -> none  [the longest x1 16.5 us: on_device(): jnp.einsum('mlpc,mpn->lnc', parted, table_rows, preferred_element_type=jn...]
    all_gather x1 -> x0, local copies, waits for them, and re-layouts: 17.1 us -> none  [on_device(): portion = lax.all_gather(mixed_spec, 'lon', axis=0, tiled=True)]
    another operation x4 -> x0, other arithmetic: 16.9 us -> none
  transfers between devices with their start and end apart: 3 -> 0, of which waited for: 3 -> 0; matrix products, arithmetic and copies ran while one was open for 5% -> 0% of each run, Pallas kernels for 0% -> 0%
where the time goes in v1:
time: 211 us
  Pallas kernels  205 us (97%)
  local copies, waits for them, and re-layouts  6.05 us (3%)
    pallas_call x1, Pallas kernels, fast_device(): pl.pallas_call(kernel, out_shape=jax.ShapeDtypeStruct((lats, 2 * M, chann...  189 us
    pallas_call x1, Pallas kernels, fast_device(): pl.pallas_call(synthesis_kernel, grid=(lats,), out_shape=jax.ShapeDtypeSt...  16 us
    unnamed x2, local copies, waits for them, and re-layouts  4.57 us

profile of v1, /device:TPU:13, one launch (start us, length us, event | category | flops | bytes accessed | tf_op | source)
XLA Modules:
  0.0 211.1 jit_solution(4272044470794830229)
XLA Ops:
  0.0 1.5 dynamic-slice_bitcast_fusion.table
  1.5 189.0 %shard_map.46.spectrum = bf16[24,1024,256]{2,1,0:T(8,128)(2,1)} custom-call(bf16[24,360,256]{2,1,0:T(8,128)(2,1)} %refs_0_.1, bf16[32,2,256,256]{3,2,1,0:T(8,128)(2,1)} %refs_1_.1, bf16[4,4,4,64,360]{4,3,2,1,0:T(8,128)(2,1)} %constant.15.clone.refs_2_), custom_call_target="tpu_custom_call" | custom-call | flops 8000000000 | bytes 41943040 | tf_op jit(solution)/shard_map/pallas_call | solution.py:328
  190.5 0.0 copy-start
  190.5 4.6 %copy-done = bf16[24,1024,256]{2,1,0:T(8,128)(2,1)S(1)} copy-done((bf16[24,1024,256]{2,1,0:T(8,128)(2,1)S(1)}, bf16[24,1024,256]{2,1,0:T(8,128)(2,1)}, u32[]{:S(2)}) %copy-start) | copy-done | bytes 12582936
  195.1 16.0 %shard_map.47 = bf16[24,720,256]{2,1,0:T(8,128)(2,1)} custom-call(bf16[720,1024]{1,0:T(8,128)(2,1)S(1)} %dynamic-slice_bitcast_fusion.table, bf16[24,1024,256]{2,1,0:T(8,128)(2,1)S(1)} %copy-done), custom_call_target="tpu_custom_call" | custom-call | tf_op jit(solution)/shard_map/pallas_call | solution.py:354
Async XLA Ops:
  190.5 4.6 %copy-start = (bf16[24,1024,256]{2,1,0:T(8,128)(2,1)S(1)}, bf16[24,1024,256]{2,1,0:T(8,128)(2,1)}, u32[]{:S(2)}) copy-start(bf16[24,1024,256]{2,1,0:T(8,128)(2,1)} %shard_map.46.spectrum) | copy-start | bytes 37748740

commit v2 on v1

--- a/solution.py
+++ b/solution.py
@@ -11,7 +11,9 @@
 NLON = 1440
 M = 512
 ROWS = 16
-HALVES = 2
+PIECES = 4
+BACK = 2
+LATS = 4
 
 
 def analysis_table(lon_index):
@@ -101,15 +103,16 @@
     factor = np.where(mode == 0, 1.0, 2.0).astype(np.float32) * np.float32(scale)
     syn = np.stack([np.cos(angle) * factor, -np.sin(angle) * factor], 1)
     syn = syn.reshape(lon_count, lat_count, chunks, ROWS, lon_count, 2 * NLON // lon_count)
-    syn = syn.transpose(4, 5, 2, 0, 1, 3).reshape(lon_count, 2 * NLON // lon_count, 2 * M)
+    syn = syn.transpose(4, 5, 2, 0, 1, 3).reshape(lon_count, 2 * NLON // lon_count, 2, M)
+    syn = syn.transpose(0, 2, 1, 3)
     kind = jnp.bfloat16
     return ana.astype(np.float32).astype(kind), syn.astype(np.float32).astype(kind)
 
 
 def spectral_kernel(
     lats, lat_n, chunks,
-    grid_in, w_in, tab_in, full,
-    g_own, g_peer, w_buf, tab, xs, acc, xr, zr, ys, xt, yt,
+    grid_in, w_in, tab_in, syn_in, full, early,
+    syn, g_own, g_peer, w_buf, tab, xs, acc, xr, zr, ys, xt, yt,
     local_sem, place_sem, gs, gr, x_s, x_r, z_s, z_r, y_s, y_r, a_s, a_r, b_s, b_r, f_s, f_r,
 ):
     lon = lax.axis_index("lon")
@@ -121,7 +124,7 @@
     x_peer = {"lon": x_lon}
     mate = {"lon": mate_lon}
     mesh_id = pl.DeviceIdType.MESH
-    part = lats // HALVES
+    part = lats // PIECES
 
     def far(src, dst, send, recv, peer):
         return pltpu.make_async_remote_copy(
@@ -134,11 +137,12 @@
         for j, owner in enumerate((x_lon, lon)):
             loads.append(
                 pltpu.make_async_copy(
-                    tab_in.at[block, owner], tab.at[i, j], local_sem.at[2 * i + j]
+                    tab_in.at[block, owner], tab.at[i, :, j], local_sem.at[2 * i + j]
                 )
             )
     loads.append(pltpu.make_async_copy(grid_in, g_own, local_sem.at[4]))
     w_load = pltpu.make_async_copy(w_in, w_buf, local_sem.at[5])
+    syn_load = pltpu.make_async_copy(syn_in.at[lon, 0], syn, local_sem.at[6])
     for copy in loads:
         copy.start()
 
@@ -149,11 +153,12 @@
 
     g_copy = [
         far(grid_in.at[pl.ds(h * part, part)], g_peer.at[pl.ds(h * part, part)], gs.at[h], gr.at[h], mate)
-        for h in range(HALVES)
+        for h in range(PIECES)
     ]
     for copy in g_copy:
         copy.start()
     w_load.start()
+    syn_load.start()
     for copy in loads:
         copy.wait()
 
@@ -164,18 +169,24 @@
         return far(half(xs, k, h), half(xr, k, h), x_s.at[k, h], x_r.at[k, h], x_peer)
 
     def analyse(k):
-        for h in range(HALVES):
+        for h in range(PIECES):
             if k == 0:
                 g_copy[h].wait_recv()
 
             @pl.loop(h * part, (h + 1) * part)
             def _(l):
+                wide = (2 * lat_n * ROWS, tab.shape[-1])
+                value = jnp.dot(
+                    tab[0, k].reshape(wide), g_own[l], preferred_element_type=jnp.float32
+                )
+                value += jnp.dot(
+                    tab[1, k].reshape(wide), g_peer[l], preferred_element_type=jnp.float32
+                )
+                value = value.astype(jnp.bfloat16)
                 for j, out in ((0, xs), (1, acc)):
-                    value = jnp.dot(tab[0, j, k], g_own[l], preferred_element_type=jnp.float32)
-                    value += jnp.dot(tab[1, j, k], g_peer[l], preferred_element_type=jnp.float32)
-                    value = value.astype(jnp.bfloat16)
                     for owner in range(lat_n):
-                        out[k, owner, l] = value[owner * ROWS:(owner + 1) * ROWS]
+                        first = (j * lat_n + owner) * ROWS
+                        out[k, owner, l] = value[first:first + ROWS]
 
             x_copy(k, h).start()
 
@@ -189,7 +200,7 @@
         )
 
     def add_up(k):
-        for h in range(HALVES):
+        for h in range(PIECES):
             x_copy(k, h).wait_recv()
 
             @pl.loop(h * part, (h + 1) * part)
@@ -205,26 +216,32 @@
             def _(l):
                 zr[k, z * lats + h * part + l] = acc[k, z, h * part + l]
 
-    def y_copy(k, d, sending):
+    some = lats // BACK
+
+    def rows_of(k, owner, source, h):
+        first = (k * 4 + owner) * lat_n * ROWS + source * ROWS
+        return full.at[pl.ds(h * some, some), pl.ds(first, ROWS)]
+
+    def y_copy(k, h, d, sending):
         source = z if sending else (z - d + lat_n) % lat_n
         target = (z + d) % lat_n if sending else z
         return far(
-            ys.at[k, pl.ds(target * lats, lats)],
-            full.at[:, pl.ds((k * 4 + lon) * lat_n * ROWS + source * ROWS, ROWS)],
-            y_s.at[k, d - 1], y_r.at[k, d - 1], {"lat": (z + d) % lat_n},
+            ys.at[k, pl.ds(target * lats + h * some, some)],
+            rows_of(k, lon, source, h),
+            y_s.at[k, h, d - 1], y_r.at[k, h, d - 1], {"lat": (z + d) % lat_n},
         )
 
-    def place(k):
+    def place(k, h):
         return pltpu.make_async_copy(
-            ys.at[k, pl.ds(z * lats, lats)],
-            full.at[:, pl.ds((k * 4 + lon) * lat_n * ROWS + z * ROWS, ROWS)],
-            place_sem.at[k],
+            ys.at[k, pl.ds(z * lats + h * some, some)],
+            rows_of(k, lon, z, h),
+            place_sem.at[k, h],
         )
 
     tiles = lat_n * lats // 16
 
     def mix(k):
-        for h in range(HALVES):
+        for h in range(PIECES):
             for d in range(1, lat_n):
                 z_copy(k, h, d, False).wait_recv()
         if k == 0:
@@ -252,61 +269,117 @@
             value = yt[:, pl.ds(start, 16)].astype(jnp.float32)
             ys[k, pl.ds(start, 16)] = jnp.swapaxes(value, 0, 1).astype(jnp.bfloat16)
 
+        for h in range(BACK):
+            for d in range(1, lat_n):
+                y_copy(k, h, d, True).start()
+            place(k, h).start()
+
+    def block(k, h, owner):
+        first = (k * 4 + owner) * lat_n * ROWS
+        return full.at[pl.ds(h * some, some), pl.ds(first, lat_n * ROWS)]
+
+    def across(k, h, sending):
+        at = block(k, h, lon if sending else x_lon)
+        return far(at, at, a_s.at[k, h], a_r.at[k, h], x_peer)
+
+    def beside(k, h, sending):
+        at = block(k, h, lon if sending else mate_lon)
+        return far(at, at, b_s.at[k, h], b_r.at[k, h], mate)
+
+    def onward(k, h, sending):
+        at = block(k, h, x_lon if sending else 3 - lon)
+        return far(at, at, f_s.at[k, h], f_r.at[k, h], mate)
+
+    def spread(k, h):
         for d in range(1, lat_n):
-            y_copy(k, d, True).start()
-        place(k).start()
-
-    def block(k, owner):
-        return full.at[:, pl.ds((k * 4 + owner) * lat_n * ROWS, lat_n * ROWS)]
-
-    def across(k, sending):
-        at = block(k, lon if sending else x_lon)
-        return far(at, at, a_s.at[k], a_r.at[k], x_peer)
-
-    def beside(k, sending):
-        at = block(k, lon if sending else mate_lon)
-        return far(at, at, b_s.at[k], b_r.at[k], mate)
-
-    def onward(k, sending):
-        at = block(k, x_lon if sending else 3 - lon)
-        return far(at, at, f_s.at[k], f_r.at[k], mate)
-
-    def spread(k):
-        for d in range(1, lat_n):
-            y_copy(k, d, False).wait_recv()
-        place(k).wait()
-        across(k, True).start()
-        beside(k, True).start()
-
-    def forward(k):
-        across(k, False).wait_recv()
-        onward(k, True).start()
-
-    steps = []
-    for k in range(chunks):
-        steps += [(2 * k, 0, analyse, k), (2 * k + 3, 1, add_up, k), (2 * k + 6, 2, mix, k)]
-        steps += [(2 * k + 9, 3, spread, k), (2 * k + 12, 4, forward, k)]
-    for _, _, stage, k in sorted(steps, key=lambda s: (s[0], -s[1])):
-        stage(k)
-
-    for h in range(HALVES):
+            y_copy(k, h, d, False).wait_recv()
+        place(k, h).wait()
+        across(k, h, True).start()
+        beside(k, h, True).start()
+
+    def forward(k, h):
+        across(k, h, False).wait_recv()
+        onward(k, h, True).start()
+
+    def arrived(k):
+        for h in range(BACK):
+            beside(k, h, False).wait_recv()
+            onward(k, h, False).wait_recv()
+
+    def spread_all(k):
+        for h in range(BACK):
+            spread(k, h)
+
+    def forward_all(k):
+        for h in range(BACK):
+            forward(k, h)
+
+    def first_sum(part_of):
+        if part_of == 0:
+            arrived(0)
+            arrived(1)
+            syn_load.wait()
+        steps = lats // LATS // 2
+
+        def body(spectrum, out):
+            for i in range(LATS):
+                value = jnp.dot(syn[...], spectrum[i], preferred_element_type=jnp.float32)
+                out[i] = value.astype(out.dtype)
+
+        pltpu.emit_pipeline(
+            body,
+            grid=(steps,),
+            in_specs=[pl.BlockSpec((LATS, M, full.shape[2]), lambda l: (l + part_of * steps, 0, 0))],
+            out_specs=[pl.BlockSpec((LATS,) + early.shape[1:], lambda l: (l + part_of * steps, 0, 0))],
+        )(full, early)
+
+    analyse(0)
+    analyse(1)
+    add_up(0)
+    analyse(2)
+    add_up(1)
+    analyse(3)
+    mix(0)
+    add_up(2)
+    mix(1)
+    spread_all(0)
+    add_up(3)
+    mix(2)
+    spread_all(1)
+    forward_all(0)
+    mix(3)
+    forward_all(1)
+    first_sum(0)
+    spread(2, 0)
+    first_sum(1)
+    for h in range(1, BACK):
+        spread(2, h)
+    for h in range(BACK):
+        spread(3, h)
+        forward(2, h)
+    forward_all(3)
+
+    for h in range(PIECES):
         g_copy[h].wait_send()
     for k in range(chunks):
-        for h in range(HALVES):
+        for h in range(PIECES):
             x_copy(k, h).wait_send()
             for d in range(1, lat_n):
                 z_copy(k, h, d, True).wait_send()
-        for d in range(1, lat_n):
-            y_copy(k, d, True).wait_send()
-        across(k, True).wait_send()
-        beside(k, True).wait_send()
-        beside(k, False).wait_recv()
-        onward(k, True).wait_send()
-        onward(k, False).wait_recv()
-
-
-def synthesis_kernel(table, spectrum, out):
-    out[0] = jnp.dot(table[...], spectrum[0], preferred_element_type=jnp.float32).astype(out.dtype)
+        for h in range(BACK):
+            for d in range(1, lat_n):
+                y_copy(k, h, d, True).wait_send()
+            across(k, h, True).wait_send()
+            beside(k, h, True).wait_send()
+            onward(k, h, True).wait_send()
+    arrived(2)
+    arrived(3)
+
+
+def synthesis_kernel(rank, table, spectrum, early, out):
+    for i in range(LATS):
+        value = jnp.dot(table[0, 0], spectrum[i], preferred_element_type=jnp.float32)
+        out[i] = (value + early[i].astype(jnp.float32)).astype(out.dtype)
 
 
 def fast_device(grid_field, weights, ana, syn):
@@ -319,49 +392,57 @@
     chunk = pltpu.VMEM((chunks, lat_n, lats, ROWS, channels), kind)
     owned = pltpu.VMEM((chunks, lat_n * lats, ROWS, channels), kind)
     turned = pltpu.VMEM((ROWS, lat_n * lats, channels), kind)
-    pair = dma((chunks, HALVES))
-    line = dma((chunks,))
+    pair = dma((chunks, PIECES))
 
     def kernel(*refs):
         spectral_kernel(lats, lat_n, chunks, *refs)
 
-    full = pl.pallas_call(
+    out_dev = syn.shape[2]
+    back = dma((chunks, BACK))
+    full, early = pl.pallas_call(
         kernel,
-        out_shape=jax.ShapeDtypeStruct((lats, 2 * M, channels), kind),
-        in_specs=[pl.BlockSpec(memory_space=pl.ANY)] * 3,
-        out_specs=pl.BlockSpec(memory_space=pl.ANY),
+        out_shape=[
+            jax.ShapeDtypeStruct((lats, 2 * M, channels), kind),
+            jax.ShapeDtypeStruct((lats, out_dev, channels), kind),
+        ],
+        in_specs=[pl.BlockSpec(memory_space=pl.ANY)] * 4,
+        out_specs=[pl.BlockSpec(memory_space=pl.ANY)] * 2,
         scratch_shapes=[
+            pltpu.VMEM((out_dev, M), kind),
             pltpu.VMEM((lats, lon_dev, channels), kind),
             pltpu.VMEM((lats, lon_dev, channels), kind),
             pltpu.VMEM(weights.shape, kind),
-            pltpu.VMEM((2, 2) + ana.shape[2:], kind),
+            pltpu.VMEM((2, chunks, 2) + ana.shape[3:], kind),
             chunk, chunk, chunk, owned, owned, turned, turned,
-            dma((6,)), line, dma((HALVES,)), dma((HALVES,)),
+            dma((7,)), back, dma((PIECES,)), dma((PIECES,)),
             pair, pair,
-            dma((chunks, HALVES, lat_n - 1)), dma((chunks, HALVES, lat_n - 1)),
-            dma((chunks, lat_n - 1)), dma((chunks, lat_n - 1)),
-            line, line, line, line, line, line,
+            dma((chunks, PIECES, lat_n - 1)), dma((chunks, PIECES, lat_n - 1)),
+            dma((chunks, BACK, lat_n - 1)), dma((chunks, BACK, lat_n - 1)),
+            back, back, back, back, back, back,
         ],
         compiler_params=pltpu.CompilerParams(
             collective_id=0, has_side_effects=True, vmem_limit_bytes=56 * 2**20
         ),
         cost_estimate=pl.CostEstimate(
-            flops=8 * 10**9, bytes_accessed=40 * 2**20, transcendentals=0
+            flops=12 * 10**9, bytes_accessed=60 * 2**20, transcendentals=0
         ),
-    )(grid_field, weights, ana)
-    table = lax.dynamic_index_in_dim(syn, lax.axis_index("lon"), 0, keepdims=False)
-    out_dev = table.shape[0]
+    )(grid_field, weights, ana, syn)
+    rank = lax.axis_index("lon").astype(jnp.int32).reshape(1)
     return pl.pallas_call(
         synthesis_kernel,
-        grid=(lats,),
+        grid_spec=pltpu.PrefetchScalarGridSpec(
+            num_scalar_prefetch=1,
+            grid=(lats // LATS,),
+            in_specs=[
+                pl.BlockSpec((1, 1, out_dev, M), lambda l, r: (r[0], 1, 0, 0)),
+                pl.BlockSpec((LATS, M, channels), lambda l, r: (l, 1, 0)),
+                pl.BlockSpec((LATS, out_dev, channels), lambda l, r: (l, 0, 0)),
+            ],
+            out_specs=pl.BlockSpec((LATS, out_dev, channels), lambda l, r: (l, 0, 0)),
+        ),
         out_shape=jax.ShapeDtypeStruct((lats, out_dev, channels), kind),
-        in_specs=[
-            pl.BlockSpec(table.shape, lambda l: (0, 0)),
-            pl.BlockSpec((1, 2 * M, channels), lambda l: (l, 0, 0)),
-        ],
-        out_specs=pl.BlockSpec((1, out_dev, channels), lambda l: (l, 0, 0)),
-        compiler_params=pltpu.CompilerParams(vmem_limit_bytes=40 * 2**20),
-    )(table, full)
+        compiler_params=pltpu.CompilerParams(vmem_limit_bytes=60 * 2**20),
+    )(rank, syn, full, early)
 
 
 def solution(mesh):

time: 211 us -> 195 us (0.924)
  Pallas kernels: 205 us -> 194 us
  local copies, waits for them, and re-layouts: 6.05 us -> 0 us
    pallas_call x2, Pallas kernels: 205 us -> 194 us  [the longest x1 182 us: fast_device(): pl.pallas_call(kernel, out_shape=[jax.ShapeDtypeStruct((lats, 2 * M, chan...]
    unnamed x2 -> x0, local copies, waits for them, and re-layouts: 4.57 us -> none
where the time goes in v2:
time: 195 us; the launch traced here: 194 us
  Pallas kernels  194 us (99%)
    pallas_call x1, Pallas kernels, fast_device(): pl.pallas_call(kernel, out_shape=[jax.ShapeDtypeStruct((lats, 2 * M, chan...  182 us
    pallas_call x1, Pallas kernels, fast_device(): pl.pallas_call(synthesis_kernel, grid_spec=pltpu.PrefetchScalarGridSpec(n...  12.3 us

profile of v2, /device:TPU:13, one launch (start us, length us, event | category | flops | bytes accessed | tf_op | source)
XLA Modules:
  0.0 194.4 jit_solution(10592807748484673370)
XLA Ops:
  0.0 182.0 %shard_map.46 = (bf16[24,1024,256]{2,1,0:T(8,128)(2,1)}, bf16[24,720,256]{2,1,0:T(8,128)(2,1)}) custom-call(bf16[24,360,256]{2,1,0:T(8,128)(2,1)} %refs_0_.1, bf16[32,2,256,256]{3,2,1,0:T(8,128)(2,1)} %refs_1_.1, bf16[4,4,4,64,360]{4,3,2,1,0:T(8,128)(2,1)} %constant.9.clone.refs_2_, bf16[4,2,720,512]{3,2,1,0:T(8,128)(2,1)} %constant.10.clone.refs_3_.table), custom_call_target="tpu_custom_call" | custom-call | flops 12000000000 | bytes 62914560 | tf_op jit(solution)/shard_map/pallas_call | solution.py:402
  182.0 12.3 %shard_map.47 = bf16[24,720,256]{2,1,0:T(8,128)(2,1)} custom-call(s32[1]{0:T(128)} %bitcast.rank, bf16[4,2,720,512]{3,2,1,0:T(8,128)(2,1)} %constant.10.clone.refs_3_.table, bf16[24,1024,256]{2,1,0:T(8,128)(2,1)} %get-tuple-element.7.spectrum, bf16[24,720,256]{2,1,0:T(8,128)(2,1)} %get-tuple-element.8.early), custom_call_target="tpu_custom_call" | custom-call | tf_op jit(solution)/shard_map/pallas_call | solution.py:431

commit v3 on v2

--- a/solution.py
+++ b/solution.py
@@ -13,6 +13,7 @@
 ROWS = 16
 PIECES = 4
 BACK = 2
+LAST = 6
 LATS = 4
 
 
@@ -349,14 +350,12 @@
     forward_all(0)
     mix(3)
     forward_all(1)
+    spread_all(2)
     first_sum(0)
-    spread(2, 0)
-    first_sum(1)
-    for h in range(1, BACK):
-        spread(2, h)
     for h in range(BACK):
         spread(3, h)
         forward(2, h)
+    first_sum(1)
     forward_all(3)
 
     for h in range(PIECES):
@@ -377,7 +376,7 @@
 
 
 def synthesis_kernel(rank, table, spectrum, early, out):
-    for i in range(LATS):
+    for i in range(LAST):
         value = jnp.dot(table[0, 0], spectrum[i], preferred_element_type=jnp.float32)
         out[i] = (value + early[i].astype(jnp.float32)).astype(out.dtype)
 
@@ -432,13 +431,15 @@
         synthesis_kernel,
         grid_spec=pltpu.PrefetchScalarGridSpec(
             num_scalar_prefetch=1,
-            grid=(lats // LATS,),
+            grid=(lats // LAST,),
             in_specs=[
                 pl.BlockSpec((1, 1, out_dev, M), lambda l, r: (r[0], 1, 0, 0)),
-                pl.BlockSpec((LATS, M, channels), lambda l, r: (l, 1, 0)),
-                pl.BlockSpec((LATS, out_dev, channels), lambda l, r: (l, 0, 0)),
+                pl.BlockSpec((LAST, M, channels), lambda l, r: (l, 1, 0)),
+                pl.BlockSpec(
+                    (LAST, out_dev, channels), lambda l, r: (l, 0, 0)
+                ),
             ],
-            out_specs=pl.BlockSpec((LATS, out_dev, channels), lambda l, r: (l, 0, 0)),
+            out_specs=pl.BlockSpec((LAST, out_dev, channels), lambda l, r: (l, 0, 0)),
         ),
         out_shape=jax.ShapeDtypeStruct((lats, out_dev, channels), kind),
         compiler_params=pltpu.CompilerParams(vmem_limit_bytes=60 * 2**20),

time: 195 us -> 189 us (0.969)
  Pallas kernels: 194 us -> 189 us
    pallas_call x1, Pallas kernels: 182 us -> 177 us  [fast_device(): pl.pallas_call(kernel, out_shape=[jax.ShapeDtypeStruct((lats, 2 * M, chan...]
where the time goes in v3:
time: 189 us
  Pallas kernels  189 us (100%)
    pallas_call x1, Pallas kernels, fast_device(): pl.pallas_call(kernel, out_shape=[jax.ShapeDtypeStruct((lats, 2 * M, chan...  177 us
    pallas_call x1, Pallas kernels, fast_device(): pl.pallas_call(synthesis_kernel, grid_spec=pltpu.PrefetchScalarGridSpec(n...  11.3 us

profile of v3, /device:TPU:13, one launch (start us, length us, event | category | flops | bytes accessed | tf_op | source)
XLA Modules:
  0.0 188.7 jit_solution(11348535334584911821)
XLA Ops:
  0.0 177.4 %shard_map.46 = (bf16[24,1024,256]{2,1,0:T(8,128)(2,1)}, bf16[24,720,256]{2,1,0:T(8,128)(2,1)}) custom-call(bf16[24,360,256]{2,1,0:T(8,128)(2,1)} %refs_0_.1, bf16[32,2,256,256]{3,2,1,0:T(8,128)(2,1)} %refs_1_.1, bf16[4,4,4,64,360]{4,3,2,1,0:T(8,128)(2,1)} %constant.9.clone.refs_2_, bf16[4,2,720,512]{3,2,1,0:T(8,128)(2,1)} %constant.10.clone.refs_3_.table), custom_call_target="tpu_custom_call" | custom-call | flops 12000000000 | bytes 62914560 | tf_op jit(solution)/shard_map/pallas_call | solution.py:401
  177.4 11.3 %shard_map.47 = bf16[24,720,256]{2,1,0:T(8,128)(2,1)} custom-call(s32[1]{0:T(128)} %bitcast.rank, bf16[4,2,720,512]{3,2,1,0:T(8,128)(2,1)} %constant.10.clone.refs_3_.table, bf16[24,1024,256]{2,1,0:T(8,128)(2,1)} %get-tuple-element.7.spectrum, bf16[24,720,256]{2,1,0:T(8,128)(2,1)} %get-tuple-element.8.early), custom_call_target="tpu_custom_call" | custom-call | tf_op jit(solution)/shard_map/pallas_call | solution.py:430
